TPU v7x, 128 devices: a whole 4x4x4 slice. The times are simulated.
128 devices in a mesh: tm: 8 (over x_lo, y), feat: 16 (over z, x_hi, core).
Axes of the slice: x: 4 (x_hi: 2, x_lo: 2; x = x_hi * 2 + x_lo), y: 4, z: 4, core: 2. Of those that a mesh axis runs over, the one named last changes fastest.
Arguments:
- dictionary: bfloat16 [16384, 16384], P('tm', 'feat'), may hold values from -6 to 6
- eigvecs: bfloat16 [16384, 256], P('feat'), may hold values from -0.046875 to 0.046875
- snapshots: float32 [32768, 16384], P('feat', 'tm'), may hold values from -0.046875 to 0.046875
Outputs:
- modes: float32 [32768, 256], P(('feat', 'tm'))
All inputs are finite; a program needn't handle non-finite values.
Results may differ from a plain program's by a relative error of at most 0.0003.
Values sent between devices are 32-bit elements; how exact they have to be, the bound alone decides.
A program may use at most 64 MiB of HBM per device.

v0:
```python
import jax
import jax.numpy as jnp
from jax import lax
from jax.sharding import Mesh
from jax.sharding import PartitionSpec as P

FEAT = ("feat_0", "feat_1", "feat_2")
FEAT_TM = ("feat_0", "feat_1", "feat_2", "tm")


def filled_up(lines, count):
    spare = -len(lines) % count
    return jnp.pad(lines, [(0, spare)] + [(0, 0)] * (lines.ndim - 1))


def sent_to_all(x, axis):
    count = lax.axis_size(axis)
    return lax.all_to_all(jnp.broadcast_to(x[None], (count, *x.shape)), axis, 0, 0, tiled=True)


def laid_out(pieces, dim):
    pieces = jnp.moveaxis(pieces, 0, dim)
    lengths = pieces.shape
    return pieces.reshape(*lengths[:dim], lengths[dim] * lengths[dim + 1], *lengths[dim + 2 :])


def whole_of(x, axes, dim):
    far, near = axes
    first = sent_to_all(x, far)
    pieces = jnp.swapaxes(sent_to_all(first, near), 0, 1)
    return laid_out(pieces.reshape(-1, *x.shape), dim)


def in_blocks(x, dim, count):
    lengths = x.shape
    pieces = x.reshape(*lengths[:dim], count, lengths[dim] // count, *lengths[dim + 1 :])
    return jnp.moveaxis(pieces, dim, 0)


def sum_at_owner(x, axis, dim):
    count = lax.axis_size(axis)
    pieces = lax.all_to_all(in_blocks(x, dim, count), axis, 0, 0, tiled=True)
    return jnp.sum(pieces, axis=0)


def sum_by_axis(x, axes, dim):
    far, near = axes
    pieces = in_blocks(x, dim, lax.axis_size(far))
    nearer = sum_at_owner(pieces, near, dim + 1)
    arrived = lax.all_to_all(nearer, far, split_axis=0, concat_axis=0, tiled=True)
    return arrived.sum(axis=0)


def sum_by_parts(x, axes):
    lines = x.reshape(-1, x.shape[-1])
    padded = filled_up(lines, lax.axis_size(axes[0]) * lax.axis_size(axes[1]))
    whole = whole_of(sum_by_axis(padded, axes, 0), axes, 0)
    return lax.slice_in_dim(whole, 0, len(lines)).reshape(x.shape)


def shards(dictionary, eigvecs, snapshots):
    partial_sums = jnp.dot(dictionary, eigvecs, preferred_element_type=jnp.float32)
    coefficients = sum_by_parts(partial_sums, (("feat_0", "feat_1"), "feat_2"))
    local_modes = jnp.dot(
        snapshots, coefficients, precision=lax.Precision.HIGHEST, preferred_element_type=jnp.float32
    )
    return sum_at_owner(local_modes, "tm", 0)


def solution(mesh):
    finer = Mesh(
        mesh.devices.reshape(mesh.shape["tm"], 4, 2, 2), ("tm", "feat_0", "feat_1", "feat_2")
    )
    return jax.shard_map(
        shards,
        mesh=finer,
        in_specs=(P("tm", FEAT), P(FEAT, None), P(FEAT, "tm")),
        out_specs=P(FEAT_TM, None),
        check_vma=False,
    )
```

profile of v0, /device:TPU:1, one launch (start us, length us, event | category | flops | bytes accessed | tf_op | source)
XLA Modules:
  0.0 123.3 jit_solution(3096157356662613851)
XLA Ops:
  0.0 0.0 copy-start
  0.0 1.0 copy-done
  1.0 3.5 %fusion = f32[2048,256]{1,0:T(8,128)S(1)} fusion(bf16[2048,1024]{1,0:T(8,128)(2,1)} %param.3, bf16[1024,256]{1,0:T(8,128)(2,1)S(1)} %copy-done), kind=kOutput, calls=%fused_computation.2 | convolution fusion | flops 1073741824 | bytes 6815744 | tf_op jit(solution)/shard_map/dot_general | solution.py:62
  4.5 0.2 copy.19
  4.7 6.5 %all_to_all.25 = f32[2,8,128,256]{3,2,1,0:T(8,128)S(1)} all-to-all(f32[2,8,128,256]{3,2,1,0:T(8,128)S(1)} %bitcast.18), channel_id=1, replica_groups=mesh['tm'=8,'feat_0'=4,'feat_1'=2,'feat_2'=2] {'feat_2'}, dimensions={0} | all-to-all | bytes 4194304 | tf_op jit(solution)/shard_map/all_to_all | solution.py:42
  11.2 1.2 reduce_sum.27
  12.4 23.9 %all_to_all.26 = f32[8,128,256]{2,1,0:T(8,128)S(1)} all-to-all(f32[8,128,256]{2,1,0:T(8,128)} %reduce_sum.27), channel_id=1, replica_groups=mesh['tm'=8,'feat_0'=4,'feat_1'=2,'feat_2'=2] {'feat_0','feat_1'}, dimensions={0} | all-to-all | bytes 2097152 | tf_op jit(solution)/shard_map/all_to_all | solution.py:50
  36.3 0.1 reduce_sum.28
  36.4 0.1 broadcast_in_dim.4
  36.5 18.7 %all_to_all.27 = f32[8,128,256]{2,1,0:T(8,128)S(1)} all-to-all(f32[8,128,256]{2,1,0:T(8,128)S(1)} %broadcast_in_dim.4), channel_id=1, replica_groups=mesh['tm'=8,'feat_0'=4,'feat_1'=2,'feat_2'=2] {'feat_0','feat_1'}, dimensions={0} | all-to-all | bytes 2097152 | tf_op jit(solution)/shard_map/all_to_all | solution.py:18
  55.2 0.2 broadcast_in_dim.5
  55.4 7.4 %all_to_all.28 = f32[2,8,128,256]{3,2,1,0:T(8,128)S(1)} all-to-all(f32[2,8,128,256]{3,2,1,0:T(8,128)S(1)} %broadcast_in_dim.5), channel_id=1, replica_groups=mesh['tm'=8,'feat_0'=4,'feat_1'=2,'feat_2'=2] {'feat_2'}, dimensions={0} | all-to-all | bytes 4194304 | tf_op jit(solution)/shard_map/all_to_all | solution.py:18
  62.8 0.1 copy.10
  62.9 29.5 %fusion.1 = f32[256,2048]{1,0:T(8,128)S(1)} fusion(f32[2048,256]{1,0:T(8,128)S(1)} %bitcast.16, f32[2048,2048]{1,0:T(8,128)} %param.5), kind=kOutput, calls=%fused_computation.3 | convolution fusion | flops 12884901888 | bytes 20971520 | tf_op jit(solution)/shard_map/dot_general | solution.py:64
  92.4 0.2 copy.18
  92.6 29.7 %all_to_all.29 = f32[8,256,256]{1,2,0:T(8,128)S(1)} all-to-all(f32[8,256,256]{1,2,0:T(8,128)S(1)} %bitcast.19), channel_id=1, replica_groups=mesh['tm'=8,'feat_0'=4,'feat_1'=2,'feat_2'=2] {'tm'}, dimensions={0} | all-to-all | bytes 4194304 | tf_op jit(solution)/shard_map/all_to_all | solution.py:42
  122.3 0.1 reduce_sum.29
  122.4 0.8 copy.13
Async XLA Ops:
  0.0 1.0 copy-start
where the time goes:
time: 124 us; the launch traced here: 123 us
  blocking collectives  86.1 us (69%)
  matrix products  33 us (27%)
  local copies, waits for them, and re-layouts  2.67 us (2%)
  other arithmetic  1.44 us (1%)
    all_to_all x2, blocking collectives, sum_at_owner(): pieces = lax.all_to_all(in_blocks(x, dim, count), axis, 0, 0, tiled=True)  36.1 us
    dot_general x1, matrix products, shards(): jnp.dot(snapshots, coefficients, precision=lax.Precision.HIGHEST, preferr...  29.5 us
    all_to_all x2, blocking collectives, sent_to_all(): lax.all_to_all(jnp.broadcast_to(x[None], (count, *x.shape)), axis, 0, 0,...  26.1 us
    all_to_all x1, blocking collectives, sum_by_axis(): lax.all_to_all(nearer, far, split_axis=0, concat_axis=0, tiled=True)  23.9 us
    dot_general x1, matrix products, shards(): jnp.dot(dictionary, eigvecs, preferred_element_type=jnp.float32)  3.47 us

commit v1 on v0

v1 whole, which is shorter than its diff:
```python
import jax
import jax.numpy as jnp
from jax import lax
from jax.experimental import pallas as pl
from jax.experimental.pallas import tpu as pltpu
from jax.sharding import PartitionSpec as P

MESH = pl.DeviceIdType.MESH
F32, BF16 = jnp.float32, jnp.bfloat16
HALF = 128
BLK = 256
COPIES = 160


def at(start, size, align=None):
    return pl.ds(start if align is None else pl.multiple_of(start, align), size)


def kernel(
    d_hbm, v_hbm, s_hbm, o_ref,
    d, v, sf, s_hi, s_lo, p_sib, q, r_core, r_az, r_bx, r_ax, r_bz, cf, w, m,
    r_ya, r_xb, r_xa, r_yb, ld, ss, rs,
):
    tm, ft = lax.axis_index("tm"), lax.axis_index("feat")
    xl, y = tm // 4, tm % 4
    z, xh, c = ft // 4, (ft // 2) % 2, ft % 2

    def to_z(k):
        return {"tm": tm, "feat": ((z + k) % 4) * 4 + xh * 2 + c}

    def to_y(k):
        return {"tm": xl * 4 + (y + k) % 4, "feat": ft}

    to_xh = {"tm": tm, "feat": z * 4 + (1 - xh) * 2 + c}
    to_xl = {"tm": (1 - xl) * 4 + y, "feat": ft}
    to_core = {"tm": tm, "feat": z * 4 + xh * 2 + (1 - c)}

    used = [0]
    sent = []

    def numbers(count):
        first = used[0]
        used[0] += count
        return first

    def copy_of(src, dst, sem, device):
        return pltpu.make_async_remote_copy(
            src_ref=src, dst_ref=dst, send_sem=ss.at[sem], recv_sem=rs.at[sem],
            device_id=device, device_id_type=MESH,
        )

    def send(src, dst, device):
        copy = copy_of(src, dst, numbers(1), device)
        copy.start()
        sent.append(copy)
        return copy

    load_v = pltpu.make_async_copy(v_hbm, v, ld.at[0])
    load_v.start()

    def load_d(i):
        rows = at(((1 - c) * 4 + i) % 8 * BLK, BLK, BLK)
        return pltpu.make_async_copy(d_hbm.at[rows], d.at[rows], ld.at[1 + i])

    def load_s(i):
        rows = at(i * BLK, BLK, BLK)
        return pltpu.make_async_copy(s_hbm.at[rows], sf.at[rows], ld.at[9 + i])

    for i in range(8):
        load_d(i).start()
    for i in range(8):
        load_s(i).start()

    partners = [to_core, to_xl, to_y(1), to_y(2), to_y(3), to_xh, to_z(1), to_z(2), to_z(3)]
    barrier = pltpu.get_barrier_semaphore()
    for device in partners:
        pl.semaphore_signal(barrier, inc=1, device_id=device, device_id_type=MESH)

    load_v.wait()

    def first_product(i):
        rows = at(((1 - c) * 4 + i) % 8 * BLK, BLK, BLK)
        return jnp.dot(d[rows, :], v[...], preferred_element_type=F32)

    def sib_block(i, carry):
        load_d(i).wait()
        part = first_product(i)
        rows = at(i * BLK, BLK, BLK)
        p_sib[0, rows, :] = part[:, :HALF]
        p_sib[1, rows, :] = part[:, HALF:]
        return carry

    lax.fori_loop(0, 4, sib_block, 0)
    pl.semaphore_wait(barrier, len(partners))
    core_copies = []
    for h in range(2):
        core_copies.append([
            send(p_sib.at[h, pl.ds(k * 512, 512)], r_core.at[h, pl.ds(k * 512, 512)], to_core)
            for k in range(2)
        ])

    def own_block(i, carry):
        load_d(4 + i).wait()
        part = first_product(4 + i)
        rows = at(i * BLK, BLK, BLK)
        q[0, rows, :] = part[:, :HALF]
        q[1, rows, :] = part[:, HALF:]
        return carry

    lax.fori_loop(0, 4, own_block, 0)

    a_own = lambda: at(z * 128, 128, 128)
    a_mine = lambda: at(z * 128 + xh * 64, 64, 64)
    a_theirs = lambda: at(z * 128 + (1 - xh) * 64, 64, 64)
    b_own = lambda: at(512 + xh * 256, 256, 256)
    b_mine = lambda: at(512 + xh * 256 + z * 64, 64, 64)

    def add_core(h, k):
        core_copies[h][k].wait_recv()
        rows = pl.ds(k * 512, 512)
        q[h, rows, :] += r_core[h, rows, :]

    def scatter_1(h):
        add_core(h, 0)
        az = [
            send(q.at[h, at((z + k) % 4 * 128, 128, 128)], r_az.at[h, k - 1], to_z(k))
            for k in (2, 1, 3)
        ]
        add_core(h, 1)
        bx = send(q.at[h, at(512 + (1 - xh) * 256, 256, 256)], r_bx.at[h], to_xh)
        return az, bx

    def scatter_2(h, az, bx):
        for copy in az:
            copy.wait_recv()
        q[h, a_own(), :] += r_az[h, 0] + r_az[h, 1] + r_az[h, 2]
        ax = send(q.at[h, a_theirs()], r_ax.at[h], to_xh)
        bx.wait_recv()
        q[h, b_own(), :] += r_bx[h]
        bz = [
            send(q.at[h, at(512 + xh * 256 + (z + k) % 4 * 64, 64, 64)], r_bz.at[h, k - 1], to_z(k))
            for k in (2, 1, 3)
        ]
        return ax, bz

    def global_rows(rows):
        return at(c * 1024 + rows.start, rows.size, 64)

    def piece(h, rows, device):
        ref = cf.at[h, global_rows(rows)]
        return send(ref, ref, device)

    def gather_1(h, ax, bz):
        ax.wait_recv()
        cf[h, global_rows(a_mine()), :] = q[h, a_mine(), :] + r_ax[h]
        g = {}
        g["ax"] = piece(h, a_mine(), to_xh)
        g["az"] = [piece(h, a_mine(), to_z(k)) for k in (2, 1, 3)]
        for copy in bz:
            copy.wait_recv()
        cf[h, global_rows(b_mine()), :] = q[h, b_mine(), :] + (r_bz[h, 0] + r_bz[h, 1] + r_bz[h, 2])
        g["bz"] = [piece(h, b_mine(), to_z(k)) for k in (2, 1, 3)]
        g["bx"] = [piece(h, b_mine(), to_xh)]
        g["core"] = [piece(h, a_mine(), to_core), piece(h, b_mine(), to_core)]
        return g

    def gather_2(h, g):
        g["ax"].wait_recv()
        g["az"] += [piece(h, a_theirs(), to_z(k)) for k in (2, 1, 3)]
        g["core"].append(piece(h, a_theirs(), to_core))
        for copy, k in zip(g["bz"], (2, 1, 3)):
            copy.wait_recv()
            rows = at(512 + xh * 256 + (z + 4 - k) % 4 * 64, 64, 64)
            g["bx"].append(piece(h, rows, to_xh))
            g["core"].append(piece(h, rows, to_core))

    def gather_3(h, g):
        for copy in g["az"]:
            copy.wait_recv()
        for k in (2, 1, 3):
            g["core"].append(piece(h, at((z + k) % 4 * 128, 128, 128), to_core))
        for copy in g["bx"]:
            copy.wait_recv()
        g["core"].append(piece(h, at(512 + (1 - xh) * 256, 256, 256), to_core))
        for copy in g["core"]:
            copy.wait_recv()
        for k in range(4):
            rows = pl.ds(k * 512, 512)
            whole = cf[h, rows, :]
            high = whole.astype(BF16)
            w[h, rows, :HALF] = high
            w[h, rows, HALF:] = (whole - high.astype(F32)).astype(BF16)

    def split(first, last):
        def body(i, carry):
            load_s(i).wait()
            for k in range(4):
                rows = at(i * BLK + k * 64, 64, 64)
                whole = sf[rows, :]
                high = whole.astype(BF16)
                s_hi[rows, :] = high
                s_lo[rows, :] = (whole - high.astype(F32)).astype(BF16)
            return carry

        lax.fori_loop(first, last, body, 0)

    sems_ya = [numbers(8) for _ in range(2)]
    sems_xb = [numbers(8) for _ in range(2)]

    def block_start(a, k):
        return (((xl + a) % 2) * 4 + (y + k) % 4) * BLK

    def copy_ya(h, a, k):
        return copy_of(
            m.at[h, at(block_start(a, k), 128, 128)], r_ya.at[h, a, k - 1],
            sems_ya[h] + a * 4 + k, to_y(k),
        )

    def copy_xb(h, k):
        return copy_of(
            m.at[h, at(block_start(1, k) + 128, 128, 128)], r_xb.at[h, k], sems_xb[h] + k, to_xl
        )

    def second_product(h, first, last):
        def body(i, carry):
            a, k = 1 - i // 4, (i + 1) % 4
            start = block_start(a, k)
            rows = at(start, BLK, BLK)
            part = jnp.dot(s_hi[rows, :], w[h], preferred_element_type=F32)
            low = jnp.dot(s_lo[rows, :], w[h, :, :HALF], preferred_element_type=F32)
            m[h, rows, :] = part[:, :HALF] + (part[:, HALF:] + low)

            @pl.when(k != 0)
            def _():
                copy_ya(h, a, k).start()

            @pl.when(a == 1)
            def _():
                copy_xb(h, k).start()

            return carry

        lax.fori_loop(first, last, body, 0)

    def reduce_1(h):
        yb = []
        for k in (1, 2, 3):
            copy_xb(h, k).wait_recv()
            r_xb[h, k] += m[h, at(block_start(0, k) + 128, 128, 128), :]
            yb.append(send(r_xb.at[h, k], r_yb.at[h, k - 1], to_y(k)))
        for k in (1, 2, 3):
            copy_ya(h, 1, k).wait_recv()
        m[h, at(block_start(1, 0), 128, 128), :] += r_ya[h, 1, 0] + r_ya[h, 1, 1] + r_ya[h, 1, 2]
        xa = send(m.at[h, at(block_start(1, 0), 128, 128)], r_xa.at[h], to_xl)
        return yb, xa

    def reduce_2(h, yb, xa):
        cols = pl.ds(h * HALF, HALF)
        for k in (1, 2, 3):
            copy_ya(h, 0, k).wait_recv()
        own = m[h, at(block_start(0, 0), 128, 128), :] + (r_ya[h, 0, 0] + r_ya[h, 0, 1] + r_ya[h, 0, 2])
        xa.wait_recv()
        o_ref[pl.ds(0, 128), cols] = own + r_xa[h]
        copy_xb(h, 0).wait_recv()
        own = m[h, at(block_start(0, 0) + 128, 128, 128), :] + r_xb[h, 0]
        for copy in yb:
            copy.wait_recv()
        o_ref[pl.ds(128, 128), cols] = own + (r_yb[h, 0] + r_yb[h, 1] + r_yb[h, 2])

    first_0 = scatter_1(0)
    first_1 = scatter_1(1)
    split(0, 3)
    second_0 = scatter_2(0, *first_0)
    split(3, 5)
    g0 = gather_1(0, *second_0)
    second_1 = scatter_2(1, *first_1)
    split(5, 6)
    gather_2(0, g0)
    split(6, 7)
    g1 = gather_1(1, *second_1)
    split(7, 8)
    gather_3(0, g0)
    second_product(0, 0, 3)
    gather_2(1, g1)
    second_product(0, 3, 8)
    gather_3(1, g1)
    second_product(1, 0, 4)
    tail_0 = reduce_1(0)
    second_product(1, 4, 8)
    tail_1 = reduce_1(1)
    reduce_2(0, *tail_0)
    reduce_2(1, *tail_1)

    for copy in sent:
        copy.wait_send()
    for h in range(2):
        for k in range(4):
            copy_xb(h, k).wait_send()
            if k:
                copy_ya(h, 0, k).wait_send()
                copy_ya(h, 1, k).wait_send()
    assert used[0] <= COPIES


def shards(dictionary, eigvecs, snapshots):
    vmem = pltpu.VMEM
    return pl.pallas_call(
        kernel,
        out_shape=jax.ShapeDtypeStruct((256, 256), F32),
        in_specs=[pl.BlockSpec(memory_space=pl.ANY)] * 3,
        out_specs=pl.BlockSpec(memory_space=pltpu.VMEM),
        scratch_shapes=[
            vmem((2048, 1024), BF16),
            vmem((1024, 256), BF16),
            vmem((2048, 2048), F32),
            vmem((2048, 2048), BF16),
            vmem((2048, 2048), BF16),
            vmem((2, 1024, HALF), F32),
            vmem((2, 1024, HALF), F32),
            vmem((2, 1024, HALF), F32),
            vmem((2, 3, 128, HALF), F32),
            vmem((2, 256, HALF), F32),
            vmem((2, 64, HALF), F32),
            vmem((2, 3, 64, HALF), F32),
            vmem((2, 2048, HALF), F32),
            vmem((2, 2048, 2 * HALF), BF16),
            vmem((2, 2048, HALF), F32),
            vmem((2, 2, 3, 128, HALF), F32),
            vmem((2, 4, 128, HALF), F32),
            vmem((2, 128, HALF), F32),
            vmem((2, 3, 128, HALF), F32),
            pltpu.SemaphoreType.DMA((17,)),
            pltpu.SemaphoreType.DMA((COPIES,)),
            pltpu.SemaphoreType.DMA((COPIES,)),
        ],
        compiler_params=pltpu.CompilerParams(
            collective_id=0, has_side_effects=True, vmem_limit_bytes=58 * 2**20
        ),
        cost_estimate=pl.CostEstimate(flops=10**10, bytes_accessed=22 * 2**20, transcendentals=0),
    )(dictionary, eigvecs, snapshots)


def solution(mesh):
    return jax.shard_map(
        shards,
        mesh=mesh,
        in_specs=(P("tm", "feat"), P("feat", None), P("feat", "tm")),
        out_specs=P(("feat", "tm"), None),
        check_vma=False,
    )
```

time: 124 us -> 61.1 us (0.49)
  blocking collectives: 86.1 us -> 0 us
  Pallas kernels: 0 us -> 59.3 us
  matrix products: 33 us -> 0 us
  other arithmetic: 1.44 us -> 0 us
    all_to_all x5 -> x0, blocking collectives: 86.1 us -> none  [the longest x2 36.1 us: sum_at_owner(): pieces = lax.all_to_all(in_blocks(x, dim, count), axis, 0, 0, tiled=True)]
    pallas_call x0 -> x1, Pallas kernels: none -> 59.3 us  [shards(): pl.pallas_call(kernel, out_shape=jax.ShapeDtypeStruct((256, 256), F32), i...]
    dot_general x2 -> x0, matrix products: 33 us -> none  [the longest x1 29.5 us: shards(): jnp.dot(snapshots, coefficients, precision=lax.Precision.HIGHEST, preferr...]
    reduce_sum x3 -> x0, other arithmetic: 1.44 us -> none  [the longest x2 1.37 us: sum_at_owner(): return jnp.sum(pieces, axis=0)]
where the time goes in v1:
time: 61.1 us; the launch traced here: 61 us
  Pallas kernels  59.3 us (97%)
  local copies, waits for them, and re-layouts  1.67 us (3%)
    pallas_call x1, Pallas kernels, shards(): pl.pallas_call(kernel, out_shape=jax.ShapeDtypeStruct((256, 256), F32), i...  59.3 us
    unnamed x1, local copies, waits for them, and re-layouts  1.67 us

profile of v1, /device:TPU:1, one launch (start us, length us, event | category | flops | bytes accessed | tf_op | source)
XLA Modules:
  0.0 61.0 jit_solution(11758176698477219446)
XLA Ops:
  0.0 59.3 %shard_map.37 = f32[256,256]{1,0:T(8,128)} custom-call(bf16[2048,1024]{1,0:T(8,128)(2,1)} %d_hbm.1, bf16[1024,256]{1,0:T(8,128)(2,1)} %v_hbm.1, f32[2048,2048]{1,0:T(8,128)} %s_hbm.1), custom_call_target="tpu_custom_call" | custom-call | flops 10000000000 | bytes 23068672 | tf_op jit(solution)/shard_map/pallas_call | solution.py:307
  59.3 1.7 %copy.5 = f32[256,256]{1,0:T(8,128)} copy(f32[256,256]{1,0:T(8,128)} %shard_map.37) | data formatting | bytes 524288

commit v2 on v0

v2 whole, which is shorter than its diff:
```python
import jax
import jax.numpy as jnp
from jax import lax
from jax.experimental import pallas as pl
from jax.experimental.pallas import tpu as pltpu
from jax.sharding import PartitionSpec as P

MESH = pl.DeviceIdType.MESH
F32, BF16 = jnp.float32, jnp.bfloat16
HALF = 128
BLK = 256
TALL = 512
EVENTS = 34
RING = (2, 1, 3)


def at(start, size, align):
    return pl.ds(pl.multiple_of(start, align), size)


def kernel(
    d_hbm, v_hbm, s_hbm, o_ref,
    d, v, sf, s_hi, s_lo, p_sib, q, r_core, r_az, r_bx, r_ax, r_bz, cf, w, m,
    r_ya, r_xb, r_xa, r_yb, ld, ss, rs,
):
    tm, ft = lax.axis_index("tm"), lax.axis_index("feat")
    xl, y = tm // 4, tm % 4
    z, xh, c = ft // 4, (ft // 2) % 2, ft % 2

    def to_z(k):
        return {"tm": tm, "feat": ((z + k) % 4) * 4 + xh * 2 + c}

    def to_y(k):
        return {"tm": xl * 4 + (y + k) % 4, "feat": ft}

    to_xh = {"tm": tm, "feat": z * 4 + (1 - xh) * 2 + c}
    to_xl = {"tm": (1 - xl) * 4 + y, "feat": ft}
    to_core = {"tm": tm, "feat": z * 4 + xh * 2 + (1 - c)}

    events = {}
    rows_sent = [0]

    def event(*name):
        return rs.at[events.setdefault(name, len(events))]

    def send(src, dst, device, *name, count=True):
        if count:
            rows_sent[0] += src.shape[0]
        pltpu.make_async_remote_copy(
            src_ref=src, dst_ref=dst, send_sem=ss.at[0], recv_sem=event(*name),
            device_id=device, device_id_type=MESH,
        ).start()

    def arrived(like, *name):
        pltpu.make_async_copy(like, like, event(*name)).wait()

    load_v = pltpu.make_async_copy(v_hbm, v, ld.at[0])

    def load_d(i):
        rows = at((2 * (1 - c) + i) % 4 * TALL, TALL, TALL)
        return pltpu.make_async_copy(d_hbm.at[rows], d.at[rows], ld.at[1 + i])

    def cells(i):
        a, k = 1 - i // 4, (i + 1) % 4
        return a, k, at((((xl + a) % 2) * 4 + (y + k) % 4) * BLK, BLK, BLK)

    def load_s(i):
        return pltpu.make_async_copy(
            s_hbm.at[cells(i)[2]], sf.at[pl.ds(i * BLK, BLK)], ld.at[5 + i // 2]
        )

    partners = [to_core, to_xl, to_y(1), to_y(2), to_y(3), to_xh, to_z(1), to_z(2), to_z(3)]
    barrier = pltpu.get_barrier_semaphore()
    for device in partners:
        pl.semaphore_signal(barrier, inc=1, device_id=device, device_id_type=MESH)
    load_v.start()
    for i in range(4):
        load_d(i).start()
    for i in range(8):
        load_s(i).start()

    def first_product(i, out, j):
        load_d(i).wait()
        rows = at((2 * (1 - c) + i) % 4 * TALL, TALL, TALL)
        part = jnp.dot(d[rows, :], v[...], preferred_element_type=F32)
        out[0, pl.ds(j * TALL, TALL), :] = part[:, :HALF]
        out[1, pl.ds(j * TALL, TALL), :] = part[:, HALF:]

    load_v.wait()
    first_product(0, p_sib, 0)
    pl.semaphore_wait(barrier, len(partners))

    def send_core(h, j):
        rows = pl.ds(j * TALL, TALL)
        send(p_sib.at[h, rows], r_core.at[h, rows], to_core, "core", h, j)

    send_core(0, 0)
    first_product(1, p_sib, 1)
    send_core(0, 1)
    send_core(1, 0)
    send_core(1, 1)
    first_product(2, q, 0)
    first_product(3, q, 1)

    def add_core(h, j):
        rows = pl.ds(j * TALL, TALL)
        arrived(r_core.at[h, rows], "core", h, j)
        q[h, rows, :] += r_core[h, rows, :]

    a_own = at(z * 128, 128, 128)
    a_mine = at(z * 128 + xh * 64, 64, 64)
    a_theirs = at(z * 128 + (1 - xh) * 64, 64, 64)
    b_own = at(512 + xh * 256, 256, 256)
    b_theirs = at(512 + (1 - xh) * 256, 256, 256)

    def b_at(k):
        return at(512 + xh * 256 + (z + k) % 4 * 64, 64, 64)

    def scatter_1(h):
        add_core(h, 0)
        for k in RING:
            send(q.at[h, at((z + k) % 4 * 128, 128, 128)], r_az.at[h, k - 1], to_z(k), "az", h)
        add_core(h, 1)
        send(q.at[h, b_theirs], r_bx.at[h], to_xh, "bx", h)

    def scatter_2(h):
        arrived(r_az.at[h], "az", h)
        q[h, a_own, :] += r_az[h, 0] + r_az[h, 1] + r_az[h, 2]
        send(q.at[h, a_theirs], r_ax.at[h], to_xh, "ax", h)
        arrived(r_bx.at[h], "bx", h)
        q[h, b_own, :] += r_bx[h]
        for k in RING:
            send(q.at[h, b_at(k)], r_bz.at[h, k - 1], to_z(k), "bz", h)

    def whole_rows(rows):
        return at(c * 1024 + rows.start, rows.size, 64)

    def share(h, rows, device, *name):
        ref = cf.at[h, whole_rows(rows)]
        send(ref, ref, device, *name)

    def gather_1(h):
        arrived(r_ax.at[h], "ax", h)
        cf[h, whole_rows(a_mine), :] = q[h, a_mine, :] + r_ax[h]
        share(h, a_mine, to_xh, "gax", h)
        for k in RING:
            share(h, a_mine, to_z(k), "gaz", h)
        arrived(r_bz.at[h], "bz", h)
        cf[h, whole_rows(b_at(0)), :] = q[h, b_at(0), :] + (r_bz[h, 0] + r_bz[h, 1] + r_bz[h, 2])
        for k in RING:
            share(h, b_at(0), to_z(k), "gbz", h)
        share(h, b_at(0), to_xh, "gbx", h)

    def gather_2(h):
        arrived(r_ax.at[h], "gax", h)
        for k in RING:
            share(h, a_theirs, to_z(k), "gaz", h)
        arrived(r_bz.at[h], "gbz", h)
        for k in RING:
            share(h, b_at(k), to_xh, "gbx", h)
        share(h, a_own, to_core, "gcore", h)
        share(h, b_own, to_core, "gcore", h)

    def gather_3(h):
        arrived(r_az.at[h], "gaz", h)
        for k in RING:
            share(h, at((z + k) % 4 * 128, 128, 128), to_core, "gcore", h)
        arrived(r_bx.at[h], "gbx", h)
        share(h, b_theirs, to_core, "gcore", h)

    def gather_4(h):
        arrived(r_core.at[h], "gcore", h)
        for k in range(4):
            rows = pl.ds(k * TALL, TALL)
            whole = cf[h, rows, :]
            high = whole.astype(BF16)
            w[h, rows, :HALF] = high
            w[h, rows, HALF:] = (whole - high.astype(F32)).astype(BF16)

    def split(j):
        load_s(2 * j).wait()
        load_s(2 * j + 1).wait()

        def body(i, carry):
            rows = at(j * TALL + i * 64, 64, 64)
            whole = sf[rows, :]
            high = whole.astype(BF16)
            s_hi[rows, :] = high
            s_lo[rows, :] = (whole - high.astype(F32)).astype(BF16)
            return carry

        lax.fori_loop(0, TALL // 64, body, 0)

    def second_product(h, first, last):
        for j in (0, 1, 2, 3):
            event("ya", h, j // 2)
            event("xb", h, j % 2)
        if first == 0:
            rows_sent[0] += 10 * 128

        def body(j, carry):
            rows = at(j * TALL, TALL, TALL)
            part = jnp.dot(s_hi[rows, :], w[h], preferred_element_type=F32)
            low = jnp.dot(s_lo[rows, :], w[h, :, :HALF], preferred_element_type=F32)
            m[h, rows, :] = part[:, :HALF] + (part[:, HALF:] + low)

            for a in (0, 1):

                @pl.when(j // 2 == 1 - a)
                def _():
                    for t in (0, 1):
                        k = (2 * j + t + 1) % 4

                        @pl.when(k != 0)
                        def _():
                            send(
                                m.at[h, at(j * TALL + t * BLK, 128, 128)], r_ya.at[h, a, k - 1],
                                to_y(k), "ya", h, a, count=False,
                            )

            for n in (0, 1):

                @pl.when(j == n)
                def _():
                    for t in (0, 1):
                        send(
                            m.at[h, pl.ds(n * TALL + t * BLK + 128, 128)], r_xb.at[h, 2 * n + t],
                            to_xl, "xb", h, n, count=False,
                        )

            return carry

        lax.fori_loop(first, last, body, 0)

    def reduce_1(h):
        for n in (0, 1):
            arrived(r_xb.at[h, pl.ds(2 * n, 2)], "xb", h, n)
            for i in ((0, 1), (2,))[n]:
                r_xb[h, i] += m[h, pl.ds((4 + i) * BLK + 128, 128), :]
                send(r_xb.at[h, i], r_yb.at[h, i], to_y(i + 1), "yb", h)
        arrived(r_ya.at[h, 1], "ya", h, 1)
        mine = pl.ds(3 * BLK, 128)
        m[h, mine, :] += r_ya[h, 1, 0] + r_ya[h, 1, 1] + r_ya[h, 1, 2]
        send(m.at[h, mine], r_xa.at[h], to_xl, "xa", h)

    def reduce_2(h):
        cols = pl.ds(h * HALF, HALF)
        arrived(r_ya.at[h, 0], "ya", h, 0)
        own = m[h, pl.ds(7 * BLK, 128), :] + (r_ya[h, 0, 0] + r_ya[h, 0, 1] + r_ya[h, 0, 2])
        arrived(r_xa.at[h], "xa", h)
        o_ref[pl.ds(0, 128), cols] = own + r_xa[h]
        own = m[h, pl.ds(7 * BLK + 128, 128), :] + r_xb[h, 3]
        arrived(r_yb.at[h], "yb", h)
        o_ref[pl.ds(128, 128), cols] = own + (r_yb[h, 0] + r_yb[h, 1] + r_yb[h, 2])

    scatter_1(0)
    scatter_1(1)
    split(0)
    scatter_2(0)
    split(1)
    scatter_2(1)
    gather_1(0)
    split(2)
    gather_1(1)
    gather_2(0)
    split(3)
    gather_2(1)
    gather_3(0)
    gather_4(0)
    second_product(0, 0, 2)
    gather_3(1)
    second_product(0, 2, 4)
    gather_4(1)
    second_product(1, 0, 2)
    reduce_1(0)
    second_product(1, 2, 4)
    reduce_1(1)
    reduce_2(0)
    reduce_2(1)

    everything = sf.at[pl.ds(0, rows_sent[0] // 16)]
    pltpu.make_async_copy(everything, everything, ss.at[0]).wait()
    assert len(events) == EVENTS and rows_sent[0] % 128 == 0


def shards(dictionary, eigvecs, snapshots):
    vmem = pltpu.VMEM
    return pl.pallas_call(
        kernel,
        out_shape=jax.ShapeDtypeStruct((256, 256), F32),
        in_specs=[pl.BlockSpec(memory_space=pl.ANY)] * 3,
        out_specs=pl.BlockSpec(memory_space=pltpu.VMEM),
        scratch_shapes=[
            vmem((2048, 1024), BF16),
            vmem((1024, 256), BF16),
            vmem((2048, 2048), F32),
            vmem((2048, 2048), BF16),
            vmem((2048, 2048), BF16),
            vmem((2, 1024, HALF), F32),
            vmem((2, 1024, HALF), F32),
            vmem((2, 1024, HALF), F32),
            vmem((2, 3, 128, HALF), F32),
            vmem((2, 256, HALF), F32),
            vmem((2, 64, HALF), F32),
            vmem((2, 3, 64, HALF), F32),
            vmem((2, 2048, HALF), F32),
            vmem((2, 2048, 2 * HALF), BF16),
            vmem((2, 2048, HALF), F32),
            vmem((2, 2, 3, 128, HALF), F32),
            vmem((2, 4, 128, HALF), F32),
            vmem((2, 128, HALF), F32),
            vmem((2, 3, 128, HALF), F32),
            pltpu.SemaphoreType.DMA((9,)),
            pltpu.SemaphoreType.DMA((1,)),
            pltpu.SemaphoreType.DMA((EVENTS,)),
        ],
        compiler_params=pltpu.CompilerParams(
            collective_id=0, has_side_effects=True, vmem_limit_bytes=58 * 2**20
        ),
        cost_estimate=pl.CostEstimate(flops=10**10, bytes_accessed=22 * 2**20, transcendentals=0),
    )(dictionary, eigvecs, snapshots)


def solution(mesh):
    return jax.shard_map(
        shards,
        mesh=mesh,
        in_specs=(P("tm", "feat"), P("feat", None), P("feat", "tm")),
        out_specs=P(("feat", "tm"), None),
        check_vma=False,
    )
```

time: 124 us -> 55.4 us (0.45)
  blocking collectives: 86.1 us -> 0 us
  Pallas kernels: 0 us -> 53.6 us
  matrix products: 33 us -> 0 us
  other arithmetic: 1.44 us -> 0 us
    all_to_all x5 -> x0, blocking collectives: 86.1 us -> none  [the longest x2 36.1 us: sum_at_owner(): pieces = lax.all_to_all(in_blocks(x, dim, count), axis, 0, 0, tiled=True)]
    pallas_call x0 -> x1, Pallas kernels: none -> 53.6 us  [shards(): pl.pallas_call(kernel, out_shape=jax.ShapeDtypeStruct((256, 256), F32), i...]
    dot_general x2 -> x0, matrix products: 33 us -> none  [the longest x1 29.5 us: shards(): jnp.dot(snapshots, coefficients, precision=lax.Precision.HIGHEST, preferr...]
    reduce_sum x3 -> x0, other arithmetic: 1.44 us -> none  [the longest x2 1.37 us: sum_at_owner(): return jnp.sum(pieces, axis=0)]
where the time goes in v2:
time: 55.4 us; the launch traced here: 55.3 us
  Pallas kernels  53.6 us (97%)
  local copies, waits for them, and re-layouts  1.67 us (3%)
    pallas_call x1, Pallas kernels, shards(): pl.pallas_call(kernel, out_shape=jax.ShapeDtypeStruct((256, 256), F32), i...  53.6 us
    unnamed x1, local copies, waits for them, and re-layouts  1.67 us

profile of v2, /device:TPU:1, one launch (start us, length us, event | category | flops | bytes accessed | tf_op | source)
XLA Modules:
  0.0 55.3 jit_solution(18349892119635466758)
XLA Ops:
  0.0 53.6 %shard_map.37 = f32[256,256]{1,0:T(8,128)} custom-call(bf16[2048,1024]{1,0:T(8,128)(2,1)} %d_hbm.1, bf16[1024,256]{1,0:T(8,128)(2,1)} %v_hbm.1, f32[2048,2048]{1,0:T(8,128)} %s_hbm.1), custom_call_target="tpu_custom_call" | custom-call | flops 10000000000 | bytes 23068672 | tf_op jit(solution)/shard_map/pallas_call | solution.py:288
  53.6 1.7 %copy.5 = f32[256,256]{1,0:T(8,128)} copy(f32[256,256]{1,0:T(8,128)} %shard_map.37) | data formatting | bytes 524288

commit v3 on v2

--- a/solution.py
+++ b/solution.py
@@ -10,8 +10,10 @@
 HALF = 128
 BLK = 256
 TALL = 512
-EVENTS = 34
+EVENTS = 38
 RING = (2, 1, 3)
+ORDER = (2, 1, 3, 0)
+FIRST_X = (96, 96)
 
 
 def at(start, size, align):
@@ -21,19 +23,22 @@
 def kernel(
     d_hbm, v_hbm, s_hbm, o_ref,
     d, v, sf, s_hi, s_lo, p_sib, q, r_core, r_az, r_bx, r_ax, r_bz, cf, w, m,
-    r_ya, r_xb, r_xa, r_yb, ld, ss, rs,
+    r_rl, r_ya, r_xb, r_xa, r_yb, ld, ss, rs,
 ):
     tm, ft = lax.axis_index("tm"), lax.axis_index("feat")
     xl, y = tm // 4, tm % 4
     z, xh, c = ft // 4, (ft // 2) % 2, ft % 2
 
+    def to_zx(k, n):
+        return {"tm": tm, "feat": ((z + k) % 4) * 4 + (xh + n) % 2 * 2 + c}
+
     def to_z(k):
-        return {"tm": tm, "feat": ((z + k) % 4) * 4 + xh * 2 + c}
+        return to_zx(k, 0)
 
     def to_y(k):
         return {"tm": xl * 4 + (y + k) % 4, "feat": ft}
 
-    to_xh = {"tm": tm, "feat": z * 4 + (1 - xh) * 2 + c}
+    to_xh = to_zx(0, 1)
     to_xl = {"tm": (1 - xl) * 4 + y, "feat": ft}
     to_core = {"tm": tm, "feat": z * 4 + xh * 2 + (1 - c)}
 
@@ -56,20 +61,27 @@
 
     load_v = pltpu.make_async_copy(v_hbm, v, ld.at[0])
 
+    def half_rows(n):
+        return at((xh + 1 + n) % 2 * TALL, TALL, TALL)
+
+    def first_rows(i):
+        owner = 1 - c if i < 2 else c
+        return at((owner * 2 + (xh + 1 + i) % 2) * TALL, TALL, TALL)
+
     def load_d(i):
-        rows = at((2 * (1 - c) + i) % 4 * TALL, TALL, TALL)
+        rows = first_rows(i)
         return pltpu.make_async_copy(d_hbm.at[rows], d.at[rows], ld.at[1 + i])
 
     def cells(i):
-        a, k = 1 - i // 4, (i + 1) % 4
-        return a, k, at((((xl + a) % 2) * 4 + (y + k) % 4) * BLK, BLK, BLK)
+        a, k = 1 - i // 4, ORDER[i % 4]
+        return at((((xl + a) % 2) * 4 + (y + k) % 4) * BLK, BLK, BLK)
 
     def load_s(i):
         return pltpu.make_async_copy(
-            s_hbm.at[cells(i)[2]], sf.at[pl.ds(i * BLK, BLK)], ld.at[5 + i // 2]
+            s_hbm.at[cells(i)], sf.at[pl.ds(i * BLK, BLK)], ld.at[5 + i // 2]
         )
 
-    partners = [to_core, to_xl, to_y(1), to_y(2), to_y(3), to_xh, to_z(1), to_z(2), to_z(3)]
+    partners = [to_core, to_xl, to_xh] + [to(k) for to in (to_y, to_z) for k in RING]
     barrier = pltpu.get_barrier_semaphore()
     for device in partners:
         pl.semaphore_signal(barrier, inc=1, device_id=device, device_id_type=MESH)
@@ -79,31 +91,30 @@
     for i in range(8):
         load_s(i).start()
 
-    def first_product(i, out, j):
+    def first_product(i, out):
         load_d(i).wait()
-        rows = at((2 * (1 - c) + i) % 4 * TALL, TALL, TALL)
-        part = jnp.dot(d[rows, :], v[...], preferred_element_type=F32)
-        out[0, pl.ds(j * TALL, TALL), :] = part[:, :HALF]
-        out[1, pl.ds(j * TALL, TALL), :] = part[:, HALF:]
+        part = jnp.dot(d[first_rows(i), :], v[...], preferred_element_type=F32)
+        out[0, half_rows(i), :] = part[:, :HALF]
+        out[1, half_rows(i), :] = part[:, HALF:]
 
     load_v.wait()
-    first_product(0, p_sib, 0)
+    first_product(0, p_sib)
     pl.semaphore_wait(barrier, len(partners))
 
     def send_core(h, j):
-        rows = pl.ds(j * TALL, TALL)
+        rows = half_rows(j)
         send(p_sib.at[h, rows], r_core.at[h, rows], to_core, "core", h, j)
 
     send_core(0, 0)
-    first_product(1, p_sib, 1)
+    first_product(1, p_sib)
     send_core(0, 1)
     send_core(1, 0)
     send_core(1, 1)
-    first_product(2, q, 0)
-    first_product(3, q, 1)
+    first_product(2, q)
+    first_product(3, q)
 
     def add_core(h, j):
-        rows = pl.ds(j * TALL, TALL)
+        rows = half_rows(j)
         arrived(r_core.at[h, rows], "core", h, j)
         q[h, rows, :] += r_core[h, rows, :]
 
@@ -118,9 +129,9 @@
 
     def scatter_1(h):
         add_core(h, 0)
+        add_core(h, 1)
         for k in RING:
             send(q.at[h, at((z + k) % 4 * 128, 128, 128)], r_az.at[h, k - 1], to_z(k), "az", h)
-        add_core(h, 1)
         send(q.at[h, b_theirs], r_bx.at[h], to_xh, "bx", h)
 
     def scatter_2(h):
@@ -191,12 +202,27 @@
 
         lax.fori_loop(0, TALL // 64, body, 0)
 
+    def lane(h):
+        return (BLK - FIRST_X[h]) // 2
+
+    def up(h, i):
+        return pl.ds(i * BLK, lane(h))
+
+    def down(h, i):
+        return pl.ds(i * BLK + lane(h), lane(h))
+
+    def by_y(h, i):
+        return pl.ds(i * BLK, 2 * lane(h))
+
+    def by_x(h, i):
+        return pl.ds(i * BLK + 2 * lane(h), FIRST_X[h])
+
     def second_product(h, first, last):
-        for j in (0, 1, 2, 3):
-            event("ya", h, j // 2)
-            event("xb", h, j % 2)
-        if first == 0:
-            rows_sent[0] += 10 * 128
+        top, low_end, x_rows = pl.ds(0, lane(h)), pl.ds(lane(h), lane(h)), pl.ds(0, FIRST_X[h])
+        for n in (0, 1):
+            event("rl", h, n)
+            event("ya", h, n)
+            event("xb", h, n)
 
         def body(j, carry):
             rows = at(j * TALL, TALL, TALL)
@@ -204,83 +230,104 @@
             low = jnp.dot(s_lo[rows, :], w[h, :, :HALF], preferred_element_type=F32)
             m[h, rows, :] = part[:, :HALF] + (part[:, HALF:] + low)
 
-            for a in (0, 1):
-
-                @pl.when(j // 2 == 1 - a)
-                def _():
-                    for t in (0, 1):
-                        k = (2 * j + t + 1) % 4
-
-                        @pl.when(k != 0)
-                        def _():
-                            send(
-                                m.at[h, at(j * TALL + t * BLK, 128, 128)], r_ya.at[h, a, k - 1],
-                                to_y(k), "ya", h, a, count=False,
-                            )
-
-            for n in (0, 1):
+            for n in range(first, last):
 
                 @pl.when(j == n)
                 def _():
-                    for t in (0, 1):
-                        send(
-                            m.at[h, pl.ds(n * TALL + t * BLK + 128, 128)], r_xb.at[h, 2 * n + t],
-                            to_xl, "xb", h, n, count=False,
-                        )
+                    a, i = 1 - n // 2, 2 * n
+                    if n % 2 == 0:
+                        for t, src, k in ((0, up(h, i), 1), (1, down(h, i), 3)):
+                            send(m.at[h, src], r_rl.at[h, a, t, top], to_y(k), "rl", h, a, count=False)
+                        src, dst, k = down(h, i + 1), r_ya.at[h, a, 0, low_end], 1
+                    else:
+                        src, dst, k = up(h, i), r_ya.at[h, a, 1, top], 3
+                    send(m.at[h, src], dst, to_y(k), "ya", h, a, count=False)
+                    if a == 1:
+                        for t in (i, i + 1):
+                            send(
+                                m.at[h, by_x(h, t)], r_xb.at[h, t, x_rows], to_xl,
+                                "xb", h, n, count=False,
+                            )
 
             return carry
 
         lax.fori_loop(first, last, body, 0)
-
-    def reduce_1(h):
-        for n in (0, 1):
-            arrived(r_xb.at[h, pl.ds(2 * n, 2)], "xb", h, n)
-            for i in ((0, 1), (2,))[n]:
-                r_xb[h, i] += m[h, pl.ds((4 + i) * BLK + 128, 128), :]
-                send(r_xb.at[h, i], r_yb.at[h, i], to_y(i + 1), "yb", h)
-        arrived(r_ya.at[h, 1], "ya", h, 1)
-        mine = pl.ds(3 * BLK, 128)
-        m[h, mine, :] += r_ya[h, 1, 0] + r_ya[h, 1, 1] + r_ya[h, 1, 2]
-        send(m.at[h, mine], r_xa.at[h], to_xl, "xa", h)
-
-    def reduce_2(h):
+        for n in range(first, last):
+            rows_sent[0] += (3 if n % 2 == 0 else 1) * lane(h) + (2 * FIRST_X[h] if n < 2 else 0)
+
+    def relay(h, a):
+        top, low_end = pl.ds(0, lane(h)), pl.ds(lane(h), lane(h))
+        arrived(r_rl.at[h, a, :, top], "rl", h, a)
+        i = 4 * (1 - a)
+        m[h, up(h, i + 1), :] += r_rl[h, a, 0, top, :]
+        send(m.at[h, up(h, i + 1)], r_ya.at[h, a, 0, top], to_y(1), "ya", h, a)
+        m[h, down(h, i + 2), :] += r_rl[h, a, 1, top, :]
+        send(m.at[h, down(h, i + 2)], r_ya.at[h, a, 1, low_end], to_y(3), "ya", h, a)
+
+    def reduce_x(h, n):
+        x_rows = pl.ds(0, FIRST_X[h])
+        arrived(r_xb.at[h, pl.ds(2 * n, 2), x_rows], "xb", h, n)
+        for i in ((0, 1), (2,))[n]:
+            r_xb[h, i, x_rows, :] += m[h, by_x(h, 4 + i), :]
+            send(r_xb.at[h, i, x_rows], r_yb.at[h, i, x_rows], to_y(ORDER[i]), "yb", h)
+
+    def reduce_y(h):
+        rows, mine = pl.ds(0, 2 * lane(h)), by_y(h, 3)
+        arrived(r_ya.at[h, 1, :, rows], "ya", h, 1)
+        m[h, mine, :] += r_ya[h, 1, 0, rows, :] + r_ya[h, 1, 1, rows, :]
+        send(m.at[h, mine], r_xa.at[h, rows], to_xl, "xa", h)
+
+    def reduce_end(h):
         cols = pl.ds(h * HALF, HALF)
-        arrived(r_ya.at[h, 0], "ya", h, 0)
-        own = m[h, pl.ds(7 * BLK, 128), :] + (r_ya[h, 0, 0] + r_ya[h, 0, 1] + r_ya[h, 0, 2])
-        arrived(r_xa.at[h], "xa", h)
-        o_ref[pl.ds(0, 128), cols] = own + r_xa[h]
-        own = m[h, pl.ds(7 * BLK + 128, 128), :] + r_xb[h, 3]
-        arrived(r_yb.at[h], "yb", h)
-        o_ref[pl.ds(128, 128), cols] = own + (r_yb[h, 0] + r_yb[h, 1] + r_yb[h, 2])
+        rows, x_rows = pl.ds(0, 2 * lane(h)), pl.ds(0, FIRST_X[h])
+        arrived(r_yb.at[h, :, x_rows], "yb", h)
+        own = m[h, by_x(h, 7), :] + r_xb[h, 3, x_rows, :]
+        o_ref[pl.ds(2 * lane(h), FIRST_X[h]), cols] = own + (
+            r_yb[h, 0, x_rows, :] + r_yb[h, 1, x_rows, :] + r_yb[h, 2, x_rows, :]
+        )
+        arrived(r_ya.at[h, 0, :, rows], "ya", h, 0)
+        own = m[h, by_y(h, 7), :] + (r_ya[h, 0, 0, rows, :] + r_ya[h, 0, 1, rows, :])
+        arrived(r_xa.at[h, rows], "xa", h)
+        o_ref[rows, cols] = own + r_xa[h, rows, :]
 
     scatter_1(0)
     scatter_1(1)
     split(0)
+    split(1)
+    split(2)
+    split(3)
     scatter_2(0)
-    split(1)
     scatter_2(1)
     gather_1(0)
-    split(2)
     gather_1(1)
     gather_2(0)
-    split(3)
     gather_2(1)
     gather_3(0)
     gather_4(0)
-    second_product(0, 0, 2)
+    second_product(0, 0, 1)
     gather_3(1)
-    second_product(0, 2, 4)
+    second_product(0, 1, 4)
+    relay(0, 1)
     gather_4(1)
-    second_product(1, 0, 2)
-    reduce_1(0)
-    second_product(1, 2, 4)
-    reduce_1(1)
-    reduce_2(0)
-    reduce_2(1)
+    second_product(1, 0, 1)
+    relay(0, 0)
+    reduce_x(0, 0)
+    second_product(1, 1, 2)
+    reduce_y(0)
+    reduce_x(0, 1)
+    second_product(1, 2, 3)
+    relay(1, 1)
+    second_product(1, 3, 4)
+    reduce_x(1, 0)
+    relay(1, 0)
+    reduce_x(1, 1)
+    reduce_y(1)
+    reduce_end(0)
+    reduce_end(1)
 
     everything = sf.at[pl.ds(0, rows_sent[0] // 16)]
     pltpu.make_async_copy(everything, everything, ss.at[0]).wait()
-    assert len(events) == EVENTS and rows_sent[0] % 128 == 0
+    assert len(events) == EVENTS and rows_sent[0] % 128 == 0, (len(events), rows_sent)
 
 
 def shards(dictionary, eigvecs, snapshots):
@@ -306,16 +353,17 @@
             vmem((2, 2048, HALF), F32),
             vmem((2, 2048, 2 * HALF), BF16),
             vmem((2, 2048, HALF), F32),
-            vmem((2, 2, 3, 128, HALF), F32),
+            vmem((2, 2, 2, 96, HALF), F32),
+            vmem((2, 2, 2, 192, HALF), F32),
             vmem((2, 4, 128, HALF), F32),
-            vmem((2, 128, HALF), F32),
+            vmem((2, 192, HALF), F32),
             vmem((2, 3, 128, HALF), F32),
             pltpu.SemaphoreType.DMA((9,)),
             pltpu.SemaphoreType.DMA((1,)),
             pltpu.SemaphoreType.DMA((EVENTS,)),
         ],
         compiler_params=pltpu.CompilerParams(
-            collective_id=0, has_side_effects=True, vmem_limit_bytes=58 * 2**20
+            collective_id=0, has_side_effects=True, vmem_limit_bytes=54720 * 2**10
         ),
         cost_estimate=pl.CostEstimate(flops=10**10, bytes_accessed=22 * 2**20, transcendentals=0),
     )(dictionary, eigvecs, snapshots)

time: 55.4 us -> 53.2 us (0.960)
  Pallas kernels: 53.6 us -> 52.4 us
  local copies, waits for them, and re-layouts: 1.67 us -> 0.71 us
    pallas_call x1, Pallas kernels: 53.6 us -> 52.4 us  [shards(): pl.pallas_call(kernel, out_shape=jax.ShapeDtypeStruct((256, 256), F32), i...]
    unnamed x1, local copies, waits for them, and re-layouts: 1.67 us -> 0.71 us
where the time goes in v3:
time: 53.2 us; the launch traced here: 53.1 us
  Pallas kernels  52.4 us (98%)
  local copies, waits for them, and re-layouts  0.71 us (1%)
    pallas_call x1, Pallas kernels, shards(): pl.pallas_call(kernel, out_shape=jax.ShapeDtypeStruct((256, 256), F32), i...  52.4 us

profile of v3, /device:TPU:1, one launch (start us, length us, event | category | flops | bytes accessed | tf_op | source)
XLA Modules:
  0.0 53.1 jit_solution(6558433769212381001)
XLA Ops:
  0.0 52.4 %shard_map.37 = f32[256,256]{1,0:T(8,128)S(1)} custom-call(bf16[2048,1024]{1,0:T(8,128)(2,1)} %d_hbm.1, bf16[1024,256]{1,0:T(8,128)(2,1)} %v_hbm.1, f32[2048,2048]{1,0:T(8,128)} %s_hbm.1), custom_call_target="tpu_custom_call" | custom-call | flops 10000000000 | bytes 23068672 | tf_op jit(solution)/shard_map/pallas_call | solution.py:335
  52.4 0.7 %copy.5 = f32[256,256]{1,0:T(8,128)} copy(f32[256,256]{1,0:T(8,128)S(1)} %shard_map.37) | data formatting | bytes 524288
